TPU v7x, 32 devices: a whole 2x2x4 slice. The times are simulated.
32 devices in a mesh: table: 2 (over x), image: 16 (over z, y, core).
Axes of the slice: x: 2, y: 2, z: 4, core: 2. Of those that a mesh axis runs over, the one named last changes fastest.
Arguments:
- traces: bfloat16 [512, 1920], P(('table', 'image')), may hold values from -6 to 6
- aperture: int32 [512, 4], P(('table', 'image')), may hold values from 0 to 15, all different within a row; in each aligned block of 16 rows (0 to 15, 16 to 31, ...) at most 8 rows name the same one
- bucket: int32 [512], P(('table', 'image')), may hold values from 0 to 3
- table_node: int32 [512, 4], P(('table', 'image')), may hold values from 0 to 15
- entry_gain: bfloat16 [512, 4], P(('table', 'image')), may hold values from 0.5 to 2
- travel: float32 [16, 16, 1024], P('image', None, 'table'), may hold values from 1 to 1918
- spread: float32 [16, 16, 1024], P('image', None, 'table'), may hold values from 0.1 to 1
Outputs:
- image: float32 [16, 1024], P('image', 'table')
Inputs may be any that keep to these rules, and one draw needn't show every extreme that they name: `aperture`: each trace names 4 different tiles. Among the 16 traces of one device at most 8 name the same tile, and in every draw some tile is named by exactly 8 of them.
All inputs are finite; a program needn't handle non-finite values.
Results may differ from a plain program's by a relative error of at most 0.0024.
Values may be sent and summed in bfloat16 or wider, within the bound.
A program may use at most 128 MiB of HBM per device.

v0:
```python
import math
import jax
import jax.numpy as jnp
from jax import lax
from jax.sharding import PartitionSpec as P

max_lag = 7


def antialias(trace_rows, filter_index):
    half_width = (2 + 2 * filter_index).astype(jnp.float32)[..., None]
    length = trace_rows.shape[-1]
    widths = [(0, 0)] * (trace_rows.ndim - 1) + [(max_lag, max_lag)]
    padded = jnp.pad(trace_rows, widths)
    summed = jnp.zeros(trace_rows.shape, jnp.float32)
    for sample_lag in range(-max_lag, max_lag + 1):
        ramp_weight = jnp.maximum(half_width - abs(sample_lag), 0.0) / (half_width * half_width)
        window = lax.slice_in_dim(
            padded, max_lag + sample_lag, max_lag + sample_lag + length, axis=trace_rows.ndim - 1
        )
        summed = summed + ramp_weight * window
    return summed


def interpolate(stack_tile, travel_tile, spread_tile):
    floor_value = jnp.floor(travel_tile)
    fraction = travel_tile - floor_value
    lower_index = floor_value.astype(jnp.int32)
    shifted = jnp.pad(stack_tile[:, 1:], ((0, 0), (0, 1)))
    paired = jnp.stack([stack_tile, shifted], axis=-1)
    picked = jnp.take_along_axis(paired, lower_index[:, :, None], axis=1)
    lower_value = picked[:, :, 0]
    upper_value = picked[:, :, 1]
    return jnp.sum(spread_tile * ((1.0 - fraction) * lower_value + fraction * upper_value), axis=0)


def per_device(traces, aperture, bucket, table_node, entry_gain, travel, spread):
    tiles = lax.axis_size("image")
    groups = lax.axis_size("table")
    trace_count, samples = traces.shape
    aper_count = aperture.shape[1]
    node_count = travel.shape[1]
    capacity = max(2, 2 * trace_count * aper_count // tiles)
    entries = trace_count * aper_count
    destination = aperture.reshape(entries)
    member = (destination[:, None] == jnp.arange(tiles, dtype=jnp.int32)[None, :]).astype(jnp.int32)
    earlier = jnp.cumsum(member, axis=0) - member
    slot_index = jnp.sum(earlier * member, axis=1)
    source_row = jnp.arange(entries, dtype=jnp.int32) // aper_count
    flat_nodes = table_node.reshape(entries)
    flat_gains = entry_gain.reshape(entries)
    node_slots = jnp.zeros((capacity, tiles), jnp.int32).at[slot_index, destination].set(flat_nodes)
    raw_slots = (
        jnp.zeros((capacity, tiles, samples), jnp.bfloat16)
        .at[slot_index, destination]
        .set(traces[source_row])
    )
    gain_slots = (
        jnp.zeros((capacity, tiles), jnp.bfloat16).at[slot_index, destination].set(flat_gains)
    )
    filter_slots = (
        jnp.zeros((capacity, tiles), jnp.int32).at[slot_index, destination].set(bucket[source_row])
    )
    raw_part = lax.all_to_all(raw_slots, "image", split_axis=1, concat_axis=1, tiled=True)
    gain_part = lax.all_to_all(gain_slots, "image", split_axis=1, concat_axis=1, tiled=True)
    filter_part = lax.all_to_all(filter_slots, "image", split_axis=1, concat_axis=1, tiled=True)
    node_part = lax.all_to_all(node_slots, "image", split_axis=1, concat_axis=1, tiled=True)
    filtered = antialias(raw_part.astype(jnp.float32), filter_part)
    weighted = (gain_part.astype(jnp.float32)[..., None] * filtered).astype(jnp.bfloat16)
    slot_total = tiles * capacity
    flat_values = weighted.reshape(slot_total, samples)
    node_member = (
        node_part.reshape(slot_total)[:, None] == jnp.arange(node_count, dtype=jnp.int32)[None, :]
    ).astype(jnp.bfloat16)
    stack = lax.dot_general(
        node_member, flat_values, (((0,), (0,)), ((), ())), preferred_element_type=jnp.float32
    )
    scale = 1.0 / math.sqrt(trace_count * groups * aper_count)
    summed_stack = lax.psum(stack, "table")
    return (interpolate(summed_stack, travel[0], spread[0]) * scale)[None, :]


def solution(mesh):
    in_specs = (
        P(("table", "image"), None),
        P(("table", "image"), None),
        P(("table", "image")),
        P(("table", "image"), None),
        P(("table", "image"), None),
        P("image", None, "table"),
        P("image", None, "table"),
    )
    out_specs = P("image", "table")
    return jax.shard_map(
        per_device, mesh=mesh, in_specs=in_specs, out_specs=out_specs, check_vma=False
    )
```

profile of v0, /device:TPU:0, one launch (start us, length us, event | category | flops | bytes accessed | tf_op | source)
XLA Modules:
  0.0 235.3 jit_solution(4942274203572084065)
XLA Ops:
  6.5 0.8 copy.41
  7.8 0.8 copy.46
  8.7 3.5 %scatter_fusion.1 = bf16[8,16]{1,0:T(8,128)(2,1)S(1)} fusion(bf16[8,16]{1,0:T(8,128)(2,1)S(1)} %broadcast_in_dim.11, s32[64]{0:T(128)S(1)} %fusion.25, bf16[64]{0:T(256)(128)(2,1)S(1)} %reshape.206), kind=kCustom, calls=%fused_computation.4 | custom fusion | bytes 896 | tf_op jit(solution)/shard_map/scatter | solution.py:59
  12.9 7.4 %all-to-all-start.1 = ((bf16[8,16,1]{0,2,1:T(2,128)(2,1)}), bf16[8,16,1]{0,2,1:T(2,128)(2,1)S(1)}, u32[]{:S(2)}, u32[]{:S(2)}) async-start(bf16[8,16,1]{0,2,1:T(2,128)(2,1)} %copy.47), calls=%async_computation.1 | async-start | bytes 16384 | tf_op jit(solution)/shard_map/all_to_all | solution.py:65
  20.4 1.4 gather_fusion
  21.8 3.5 %scatter_fusion.2 = s32[8,16]{1,0:T(8,128)S(1)} fusion(s32[8,16]{1,0:T(8,128)S(1)} %broadcast.222.clone, s32[64]{0:T(128)S(1)} %fusion.25, s32[64]{0:T(128)S(1)} %gather_fusion), kind=kCustom, calls=%fused_computation.5 | custom fusion | bytes 1280 | tf_op jit(solution)/shard_map/scatter | solution.py:62
  25.9 0.8 all-to-all-done.1
  26.7 5.2 %all-to-all-start.2 = ((s32[8,16,1]{0,2,1:T(1,128)}), s32[8,16,1]{0,2,1:T(1,128)S(1)}, u32[]{:S(2)}, u32[]{:S(2)}) async-start(s32[8,16,1]{0,2,1:T(1,128)} %copy.49), calls=%async_computation.2 | async-start | bytes 16384 | tf_op jit(solution)/shard_map/all_to_all | solution.py:66
  31.9 0.8 copy.43
  32.8 3.5 %scatter_fusion = s32[8,16]{1,0:T(8,128)S(1)} fusion(s32[8,16]{1,0:T(8,128)S(1)} %broadcast.222.clone.1, s32[64]{0:T(128)S(1)} %fusion.25, s32[64]{0:T(128)S(1)} %reshape.200), kind=kCustom, calls=%fused_computation.3 | custom fusion | bytes 1280 | tf_op jit(solution)/shard_map/scatter | solution.py:52
  36.9 1.4 all-to-all-done.2
  38.4 4.6 %all-to-all-start = ((s32[8,16,1]{0,2,1:T(1,128)}), s32[8,16,1]{0,2,1:T(1,128)S(1)}, u32[]{:S(2)}, u32[]{:S(2)}) async-start(s32[8,16,1]{0,2,1:T(1,128)} %copy.44), calls=%async_computation | async-start | bytes 16384 | tf_op jit(solution)/shard_map/all_to_all | solution.py:67
  43.8 6.3 %scatter_fusion.3 = bf16[8,16,1920]{2,1,0:T(8,128)(2,1)S(1)} fusion(bf16[8,16,1920]{2,1,0:T(8,128)(2,1)S(1)} %broadcast_in_dim.12, s32[64]{0:T(128)S(1)} %fusion.25, bf16[64,1920]{1,0:T(8,128)(2,1)S(1)} %gather_fusion.1), kind=kCustom, calls=%fused_computation.6 | custom fusion | bytes 737792 | tf_op jit(solution)/shard_map/scatter | solution.py:56
  50.1 0.9 copy.51
  50.9 6.0 %all-to-all-start.3 = ((bf16[8,16,1920]{2,0,1:T(8,128)(2,1)}), bf16[8,16,1920]{2,0,1:T(8,128)(2,1)S(1)}, u32[]{:S(2)}, u32[]{:S(2)}) async-start(bf16[8,16,1920]{2,0,1:T(8,128)(2,1)} %copy.51), calls=%async_computation.3 | async-start | bytes 983040 | tf_op jit(solution)/shard_map/all_to_all | solution.py:64
  57.4 13.3 %all-to-all-done.3 = bf16[8,16,1920]{2,0,1:T(8,128)(2,1)S(1)} async-done(((bf16[8,16,1920]{2,0,1:T(8,128)(2,1)}), bf16[8,16,1920]{2,0,1:T(8,128)(2,1)S(1)}, u32[]{:S(2)}, u32[]{:S(2)}) %all-to-all-start.3) | async-done | bytes 491552 | tf_op jit(solution)/shard_map/all_to_all | solution.py:64
  70.8 4.0 %multiply_convert_fusion = bf16[8,16,1920]{2,1,0:T(8,128)(2,1)S(1)} fusion(f32[8,16,1920]{2,1,0:T(8,128)S(1)} %copy_convert_fusion, f32[8,16]{1,0:T(8,128)S(1)} %get-tuple-element.6, f32[8,16]{1,0:T(8,128)S(1)} %get-tuple-element.7, f32[8,16]{1,0:T(8,128)S(1)} %get-tuple-element.8, f32[8,16]{1,0:T(8,128)S(1)} %get-tuple-element.9, ...), kind=kLoop, calls=%fused_computation.7 | loop fusion | flops 7618560 | bytes 1479168 | tf_op jit(solution)/shard_map/convert_element_type | solution.py:69
  74.8 0.9 fusion.11
  75.8 20.8 %all-reduce.4.cloned.1.call-done = f32[16,1920]{1,0:T(8,128)} async-done(((f32[16,1920]{1,0:T(8,128)}), f32[16,1920]{1,0:T(8,128)}) %all-reduce.4.cloned.1.call-update) | async-done | bytes 122896 | tf_op jit(solution)/shard_map/psum | solution.py:79
  96.6 1.0 slice.83
  97.6 0.9 pad_maximum_fusion
  98.6 7.8 %copy.53 = f32[16,1920,2]{2,1,0:T(8,128)} copy(f32[16,1920,2]{1,0,2:T(8,128)S(1)} %pad_maximum_fusion) | data formatting | bytes 491520 | tf_op jit(solution)/shard_map/stack | solution.py:30
  106.3 118.6 %gather_fusion.2 = f32[8192,2]{1,0:T(8,128)} fusion(f32[16,1920,2]{2,1,0:T(8,128)} %copy.53, s32[8192]{0:T(1024)S(1)} %bitcast.70), kind=kCustom, calls=%fused_computation.2 | custom fusion | bytes 196608 | tf_op jit(solution)/shard_map/jit(take_along_axis)/gather | solution.py:31
  225.0 2.8 %copy.54 = f32[16,512,2]{1,0,2:T(8,128)S(1)} copy(f32[16,512,2]{2,1,0:T(8,128)} %bitcast.74) | data formatting | bytes 131072 | tf_op jit(solution)/shard_map/jit(take_along_axis)/gather | solution.py:31
  (41 shorter events, 4.7 us)
Async XLA Ops:
  6.5 36.4 %copy-start = (bf16[16,1920]{1,0:T(8,128)(2,1)S(1)}, bf16[16,1920]{1,0:T(8,128)(2,1)}, u32[]{:S(2)}) copy-start(bf16[16,1920]{1,0:T(8,128)(2,1)} %param.7) | copy-start | bytes 184324
  12.9 13.8 %all-to-all-start.1 = ((bf16[8,16,1]{0,2,1:T(2,128)(2,1)}), bf16[8,16,1]{0,2,1:T(2,128)(2,1)S(1)}, u32[]{:S(2)}, u32[]{:S(2)}) async-start(bf16[8,16,1]{0,2,1:T(2,128)(2,1)} %copy.47), calls=%async_computation.1 | async-start | bytes 16384 | tf_op jit(solution)/shard_map/all_to_all | solution.py:65
  26.7 11.6 %all-to-all-start.2 = ((s32[8,16,1]{0,2,1:T(1,128)}), s32[8,16,1]{0,2,1:T(1,128)S(1)}, u32[]{:S(2)}, u32[]{:S(2)}) async-start(s32[8,16,1]{0,2,1:T(1,128)} %copy.49), calls=%async_computation.2 | async-start | bytes 16384 | tf_op jit(solution)/shard_map/all_to_all | solution.py:66
  38.4 12.6 %all-to-all-start = ((s32[8,16,1]{0,2,1:T(1,128)}), s32[8,16,1]{0,2,1:T(1,128)S(1)}, u32[]{:S(2)}, u32[]{:S(2)}) async-start(s32[8,16,1]{0,2,1:T(1,128)} %copy.44), calls=%async_computation | async-start | bytes 16384 | tf_op jit(solution)/shard_map/all_to_all | solution.py:67
  43.0 14.0 %copy-start.1 = (f32[1,16,512]{2,1,0:T(8,128)S(1)}, f32[1,16,512]{2,1,0:T(8,128)}, u32[]{:S(2)}) copy-start(f32[1,16,512]{2,1,0:T(8,128)} %param.12) | copy-start | bytes 98308
  50.9 19.8 %all-to-all-start.3 = ((bf16[8,16,1920]{2,0,1:T(8,128)(2,1)}), bf16[8,16,1920]{2,0,1:T(8,128)(2,1)S(1)}, u32[]{:S(2)}, u32[]{:S(2)}) async-start(bf16[8,16,1920]{2,0,1:T(8,128)(2,1)} %copy.51), calls=%async_computation.3 | async-start | bytes 983040 | tf_op jit(solution)/shard_map/all_to_all | solution.py:64
  56.9 39.7 %all-reduce.4.cloned.1.call-start = ((), (), s32[]{:S(2)}) async-start(), calls=%async_computation.4 | async-start | bytes 245760 | tf_op jit(solution)/shard_map/psum | solution.py:79
  225.0 2.9 %copy-start.2 = (f32[1,16,512]{2,1,0:T(8,128)S(1)}, f32[1,16,512]{2,1,0:T(8,128)}, u32[]{:S(2)}) copy-start(f32[1,16,512]{2,1,0:T(8,128)} %param.13) | copy-start | bytes 98308
Sparse Core Ops, SparseCore 0:
  75.9 20.6 all-reduce.3
where the time goes:
time: 236 us; the launch traced here: 235 us
  local copies, waits for them, and re-layouts  155 us (66%)
  waiting for transfers between devices  36.4 us (15%)
  starting transfers between devices  23.2 us (10%)
  between operations  13.6 us (6%)
  other arithmetic  6.02 us (3%)
    gather x2, local copies, waits for them, and re-layouts, interpolate(): picked = jnp.take_along_axis(paired, lower_index[:, :, None], axis=1)  121 us
    psum x1, waiting for transfers between devices, per_device(): summed_stack = lax.psum(stack, 'table')  20.8 us
    all_to_all x1, waiting for transfers between devices, per_device(): lax.all_to_all(raw_slots, 'image', split_axis=1, concat_axis=1, tiled=True)  13.3 us
    another operation x2, local copies, waits for them, and re-layouts, interpolate(): paired = jnp.stack([stack_tile, shifted], axis=-1)  7.79 us
    all_to_all x1, starting transfers between devices, per_device(): lax.all_to_all(gain_slots, 'image', split_axis=1, concat_axis=1, tiled=True)  7.39 us
    scatter x2, local copies, waits for them, and re-layouts, per_device(): raw_slots = jnp.zeros((capacity, tiles, samples), jnp.bfloat16).at[slot_i...  7.14 us
    scatter x2, local copies, waits for them, and re-layouts, per_device(): jnp.zeros((capacity, tiles), jnp.int32).at[slot_index, destination]  6.91 us
    all_to_all x1, starting transfers between devices, per_device(): lax.all_to_all(raw_slots, 'image', split_axis=1, concat_axis=1, tiled=True)  6.01 us
  transfers between devices with their start and end apart: 5, of which 4 were waited for; matrix products, arithmetic and copies ran while one was open for 8% of the time, Pallas kernels for 0%

commit v1 on v0

--- a/solution.py
+++ b/solution.py
@@ -76,7 +76,7 @@
         node_member, flat_values, (((0,), (0,)), ((), ())), preferred_element_type=jnp.float32
     )
     scale = 1.0 / math.sqrt(trace_count * groups * aper_count)
-    summed_stack = lax.psum(stack, "table")
+    summed_stack = jnp.sum(lax.all_gather(stack, "table"), axis=0)
     return (interpolate(summed_stack, travel[0], spread[0]) * scale)[None, :]
 
 

time: 236 us -> 206 us (0.87)
  waiting for transfers between devices: 36.4 us -> 15.6 us
  between operations: 13.6 us -> 0.24 us
  blocking collectives: 0 us -> 6.02 us
    psum x1 -> x0, waiting for transfers between devices: 20.8 us -> none  [per_device(): summed_stack = lax.psum(stack, 'table')]
    all_gather x0 -> x1, blocking collectives: none -> 6.02 us  [per_device(): summed_stack = jnp.sum(lax.all_gather(stack, 'table'), axis=0)]
  transfers between devices with their start and end apart: 5 -> 4, of which waited for: 4 -> 3; matrix products, arithmetic and copies ran while one was open for 8% -> 9% of each run, Pallas kernels for 0% -> 0%
where the time goes in v1:
time: 206 us; the launch traced here: 205 us
  local copies, waits for them, and re-layouts  154 us (75%)
  starting transfers between devices  23.2 us (11%)
  waiting for transfers between devices  15.6 us (8%)
  blocking collectives  6.02 us (3%)
  other arithmetic  5.14 us (2%)
    gather x2, local copies, waits for them, and re-layouts, interpolate(): picked = jnp.take_along_axis(paired, lower_index[:, :, None], axis=1)  121 us
    all_to_all x1, waiting for transfers between devices, per_device(): lax.all_to_all(raw_slots, 'image', split_axis=1, concat_axis=1, tiled=True)  13.4 us
    another operation x2, local copies, waits for them, and re-layouts, interpolate(): paired = jnp.stack([stack_tile, shifted], axis=-1)  7.79 us
    all_to_all x1, starting transfers between devices, per_device(): lax.all_to_all(gain_slots, 'image', split_axis=1, concat_axis=1, tiled=True)  7.39 us
    scatter x2, local copies, waits for them, and re-layouts, per_device(): raw_slots = jnp.zeros((capacity, tiles, samples), jnp.bfloat16).at[slot_i...  7.14 us
    scatter x2, local copies, waits for them, and re-layouts, per_device(): jnp.zeros((capacity, tiles), jnp.int32).at[slot_index, destination]  6.91 us
    all_gather x1, blocking collectives, per_device(): summed_stack = jnp.sum(lax.all_gather(stack, 'table'), axis=0)  6.02 us
    all_to_all x1, starting transfers between devices, per_device(): lax.all_to_all(raw_slots, 'image', split_axis=1, concat_axis=1, tiled=True)  6.01 us
  transfers between devices with their start and end apart: 4, of which 3 were waited for; matrix products, arithmetic and copies ran while one was open for 9% of the time, Pallas kernels for 0%

profile of v1, /device:TPU:0, one launch (start us, length us, event | category | flops | bytes accessed | tf_op | source)
XLA Modules:
  0.0 204.6 jit_solution(5882503533904131724)
XLA Ops:
  0.0 0.8 copy.48
  1.3 0.8 copy.53
  2.2 3.5 %scatter_fusion.1 = bf16[8,16]{1,0:T(8,128)(2,1)S(1)} fusion(bf16[8,16]{1,0:T(8,128)(2,1)S(1)} %broadcast_in_dim.11, s32[64]{0:T(128)S(1)} %fusion.25, bf16[64]{0:T(256)(128)(2,1)S(1)} %reshape.206), kind=kCustom, calls=%fused_computation.4 | custom fusion | bytes 896 | tf_op jit(solution)/shard_map/scatter | solution.py:59
  5.7 0.7 copy.54
  6.4 7.4 %all-to-all-start.1 = ((bf16[8,16,1]{0,2,1:T(2,128)(2,1)}), bf16[8,16,1]{0,2,1:T(2,128)(2,1)S(1)}, u32[]{:S(2)}, u32[]{:S(2)}) async-start(bf16[8,16,1]{0,2,1:T(2,128)(2,1)} %copy.54), calls=%async_computation.1 | async-start | bytes 16384 | tf_op jit(solution)/shard_map/all_to_all | solution.py:65
  13.8 1.4 gather_fusion
  15.3 3.5 %scatter_fusion.2 = s32[8,16]{1,0:T(8,128)S(1)} fusion(s32[8,16]{1,0:T(8,128)S(1)} %broadcast.222.clone, s32[64]{0:T(128)S(1)} %fusion.25, s32[64]{0:T(128)S(1)} %gather_fusion), kind=kCustom, calls=%fused_computation.5 | custom fusion | bytes 1280 | tf_op jit(solution)/shard_map/scatter | solution.py:62
  18.7 0.7 copy.56
  19.4 0.8 all-to-all-done.1
  20.2 5.2 %all-to-all-start.2 = ((s32[8,16,1]{0,2,1:T(1,128)}), s32[8,16,1]{0,2,1:T(1,128)S(1)}, u32[]{:S(2)}, u32[]{:S(2)}) async-start(s32[8,16,1]{0,2,1:T(1,128)} %copy.56), calls=%async_computation.2 | async-start | bytes 16384 | tf_op jit(solution)/shard_map/all_to_all | solution.py:66
  25.4 0.8 copy.50
  26.3 3.5 %scatter_fusion = s32[8,16]{1,0:T(8,128)S(1)} fusion(s32[8,16]{1,0:T(8,128)S(1)} %broadcast.222.clone.1, s32[64]{0:T(128)S(1)} %fusion.25, s32[64]{0:T(128)S(1)} %reshape.200), kind=kCustom, calls=%fused_computation.3 | custom fusion | bytes 1280 | tf_op jit(solution)/shard_map/scatter | solution.py:52
  30.4 1.4 all-to-all-done.2
  31.8 4.6 %all-to-all-start = ((s32[8,16,1]{0,2,1:T(1,128)}), s32[8,16,1]{0,2,1:T(1,128)S(1)}, u32[]{:S(2)}, u32[]{:S(2)}) async-start(s32[8,16,1]{0,2,1:T(1,128)} %copy.51), calls=%async_computation | async-start | bytes 16384 | tf_op jit(solution)/shard_map/all_to_all | solution.py:67
  36.4 0.8 gather_fusion.1
  37.2 6.3 %scatter_fusion.3 = bf16[8,16,1920]{2,1,0:T(8,128)(2,1)S(1)} fusion(bf16[8,16,1920]{2,1,0:T(8,128)(2,1)S(1)} %broadcast_in_dim.12, s32[64]{0:T(128)S(1)} %fusion.25, bf16[64,1920]{1,0:T(8,128)(2,1)S(1)} %gather_fusion.1), kind=kCustom, calls=%fused_computation.6 | custom fusion | bytes 737792 | tf_op jit(solution)/shard_map/scatter | solution.py:56
  43.5 0.9 copy.58
  44.4 6.0 %all-to-all-start.3 = ((bf16[8,16,1920]{2,0,1:T(8,128)(2,1)}), bf16[8,16,1920]{2,0,1:T(8,128)(2,1)S(1)}, u32[]{:S(2)}, u32[]{:S(2)}) async-start(bf16[8,16,1920]{2,0,1:T(8,128)(2,1)} %copy.58), calls=%async_computation.3 | async-start | bytes 983040 | tf_op jit(solution)/shard_map/all_to_all | solution.py:64
  50.8 13.4 %all-to-all-done.3 = bf16[8,16,1920]{2,0,1:T(8,128)(2,1)S(1)} async-done(((bf16[8,16,1920]{2,0,1:T(8,128)(2,1)}), bf16[8,16,1920]{2,0,1:T(8,128)(2,1)S(1)}, u32[]{:S(2)}, u32[]{:S(2)}) %all-to-all-start.3) | async-done | bytes 491552 | tf_op jit(solution)/shard_map/all_to_all | solution.py:64
  64.3 4.0 %multiply_convert_fusion = bf16[8,16,1920]{2,1,0:T(8,128)(2,1)S(1)} fusion(f32[8,16,1920]{2,1,0:T(8,128)S(1)} %copy_convert_fusion, f32[8,16]{1,0:T(8,128)S(1)} %get-tuple-element.6, f32[8,16]{1,0:T(8,128)S(1)} %get-tuple-element.7, f32[8,16]{1,0:T(8,128)S(1)} %get-tuple-element.8, f32[8,16]{1,0:T(8,128)S(1)} %get-tuple-element.9, ...), kind=kLoop, calls=%fused_computation.7 | loop fusion | flops 7618560 | bytes 1479168 | tf_op jit(solution)/shard_map/convert_element_type | solution.py:69
  68.5 6.0 %all-gather = f32[32,1920]{1,0:T(8,128)S(1)} all-gather(f32[16,1920]{1,0:T(8,128)S(1)} %fusion.11), channel_id=2, replica_groups=mesh['table'=2,'image'=16] {'table'}, dimensions={0}, use_global_device_ids=true | all-gather | bytes 368640 | tf_op jit(solution)/shard_map/all_gather | solution.py:79
  74.7 7.8 %copy.60 = f32[16,1920,2]{2,1,0:T(8,128)} copy(f32[16,1920,2]{1,0,2:T(8,128)S(1)} %pad_maximum_fusion) | data formatting | bytes 491520 | tf_op jit(solution)/shard_map/stack | solution.py:30
  82.5 118.6 %gather_fusion.2 = f32[8192,2]{1,0:T(8,128)} fusion(f32[16,1920,2]{2,1,0:T(8,128)} %copy.60, s32[8192]{0:T(1024)S(1)} %bitcast.71), kind=kCustom, calls=%fused_computation.2 | custom fusion | bytes 196608 | tf_op jit(solution)/shard_map/jit(take_along_axis)/gather | solution.py:31
  201.1 2.8 %copy.61 = f32[16,512,2]{1,0,2:T(8,128)S(1)} copy(f32[16,512,2]{2,1,0:T(8,128)} %bitcast.75) | data formatting | bytes 131072 | tf_op jit(solution)/shard_map/jit(take_along_axis)/gather | solution.py:31
  (40 shorter events, 3.0 us)
Async XLA Ops:
  0.0 36.4 %copy-start = (bf16[16,1920]{1,0:T(8,128)(2,1)S(1)}, bf16[16,1920]{1,0:T(8,128)(2,1)}, u32[]{:S(2)}) copy-start(bf16[16,1920]{1,0:T(8,128)(2,1)} %param.7) | copy-start | bytes 184324
  6.4 13.8 %all-to-all-start.1 = ((bf16[8,16,1]{0,2,1:T(2,128)(2,1)}), bf16[8,16,1]{0,2,1:T(2,128)(2,1)S(1)}, u32[]{:S(2)}, u32[]{:S(2)}) async-start(bf16[8,16,1]{0,2,1:T(2,128)(2,1)} %copy.54), calls=%async_computation.1 | async-start | bytes 16384 | tf_op jit(solution)/shard_map/all_to_all | solution.py:65
  20.2 11.6 %all-to-all-start.2 = ((s32[8,16,1]{0,2,1:T(1,128)}), s32[8,16,1]{0,2,1:T(1,128)S(1)}, u32[]{:S(2)}, u32[]{:S(2)}) async-start(s32[8,16,1]{0,2,1:T(1,128)} %copy.56), calls=%async_computation.2 | async-start | bytes 16384 | tf_op jit(solution)/shard_map/all_to_all | solution.py:66
  31.8 12.6 %all-to-all-start = ((s32[8,16,1]{0,2,1:T(1,128)}), s32[8,16,1]{0,2,1:T(1,128)S(1)}, u32[]{:S(2)}, u32[]{:S(2)}) async-start(s32[8,16,1]{0,2,1:T(1,128)} %copy.51), calls=%async_computation | async-start | bytes 16384 | tf_op jit(solution)/shard_map/all_to_all | solution.py:67
  36.4 14.0 %copy-start.1 = (f32[1,16,512]{2,1,0:T(8,128)S(1)}, f32[1,16,512]{2,1,0:T(8,128)}, u32[]{:S(2)}) copy-start(f32[1,16,512]{2,1,0:T(8,128)} %param.12) | copy-start | bytes 98308
  44.4 19.8 %all-to-all-start.3 = ((bf16[8,16,1920]{2,0,1:T(8,128)(2,1)}), bf16[8,16,1920]{2,0,1:T(8,128)(2,1)S(1)}, u32[]{:S(2)}, u32[]{:S(2)}) async-start(bf16[8,16,1920]{2,0,1:T(8,128)(2,1)} %copy.58), calls=%async_computation.3 | async-start | bytes 983040 | tf_op jit(solution)/shard_map/all_to_all | solution.py:64
  201.1 2.9 %copy-start.2 = (f32[1,16,512]{2,1,0:T(8,128)S(1)}, f32[1,16,512]{2,1,0:T(8,128)}, u32[]{:S(2)}) copy-start(f32[1,16,512]{2,1,0:T(8,128)} %param.13) | copy-start | bytes 98308
